TPU v7x, 1024 devices: a whole 4x8x16 slice. The times are simulated.
1024 devices in a mesh: replica: 32 (over z, y_hi), fsdp: 32 (over x, y_lo, core).
Axes of the slice: x: 4, y: 8 (y_hi: 2, y_lo: 4; y = y_hi * 4 + y_lo), z: 16, core: 2. Of those that a mesh axis runs over, the one named last changes fastest.
Arguments:
- grad: bfloat16 [256, 512, 512], P('replica', 'fsdp'), may hold values from -180 to 180
- statistics: float32 [1024, 512, 256], P(('replica', 'fsdp')), may hold values from -2000 to 2000, as said below
- moment: float32 [1024, 256, 256], P(('replica', 'fsdp')), may hold values from 0.01 to 10
- assignment: int32 [256], P('replica'), may hold values from 0 to 15, as said below
- newton_steps: int32 [256], P('replica'), may hold values from 2 to 3
Outputs:
- direction: bfloat16 [32, 32, 256, 256], P(None, 'fsdp')
- new_statistics: float32 [1024, 512, 256], P(('replica', 'fsdp'))
- new_moment: float32 [1024, 256, 256], P(('replica', 'fsdp'))
Inputs may be any that keep to these rules, and one draw needn't show every extreme that they name: `assignment`: for every replica group r, entries r * 8 to (r + 1) * 8 - 1 taken modulo 32 / 4 are a permutation of 0 to 7. `statistics`: the two factors that the column halves of each slot form are symmetric positive definite.
All inputs are finite; a program needn't handle non-finite values.
Results may differ from a plain program's by a relative error of at most 0.001.
Values may be sent and summed in bfloat16 or wider, within the bound.
A program may use at most 32 MiB of HBM per device.

v0:
```python
import jax
import jax.numpy as jnp
from jax import lax
from jax.sharding import PartitionSpec as P

NEWTON_MAX = 3


highest = lax.Precision.HIGHEST


def partner_2(block, axis, distance):
    count = lax.axis_size(axis)
    route = []
    for low in range(count):
        high = low | 1 << distance
        if high != low and high < count:
            route += [(low, high), (high, low)]
    return lax.ppermute(block, axis, route)


def product(left_part, right_part):
    return jnp.dot(left_part, right_part, precision=highest, preferred_element_type=jnp.float32)


def partner(payload_item):
    return partner_2(payload_item, "fsdp", 0)


def opposite(payload_item):
    return partner_2(payload_item, "fsdp", 1)


def assemble(own_part, other_part, half_index):
    leading = jnp.where(half_index == 0, own_part, other_part)
    trailing = jnp.where(half_index == 0, other_part, own_part)
    return jnp.concatenate([leading, trailing], axis=1)


def column_half(full_matrix, half_index, half_width):
    return lax.dynamic_slice_in_dim(full_matrix, half_index * half_width, half_width, 1)


def on_device(grad, statistics, moment, assignment, newton_steps):
    block_order = grad.shape[2]
    half_width = block_order // 2
    groups = assignment.shape[0]
    fsdp_index = lax.axis_index("fsdp")
    member = fsdp_index % 4
    half_index = member % 2
    side_index = member // 2
    slot_index = fsdp_index // 4
    local_blocks = assignment % groups
    block_picks = jnp.repeat(local_blocks, 4)
    outgoing = jnp.take(grad, block_picks, axis=0)
    incoming = lax.all_to_all(outgoing, "fsdp", split_axis=0, concat_axis=0, tiled=True)
    positions = jnp.arange(groups, dtype=jnp.int32)
    chosen_entry = jnp.sum(jnp.where(positions == slot_index, assignment, 0))
    chosen = chosen_entry % groups
    flipped = chosen_entry // groups
    received_block = incoming.reshape(block_order, block_order)
    gradient_block = jnp.where(flipped == 1, received_block.T, received_block)
    newton_count = jnp.sum(jnp.where(positions == chosen, newton_steps, 0))
    rows_own = lax.dynamic_slice_in_dim(gradient_block, half_index * half_width, half_width, 0)
    cols_own = lax.dynamic_slice_in_dim(gradient_block, half_index * half_width, half_width, 1)
    gram_half = lax.cond(
        side_index == 0,
        lambda: lax.dot_general(
            gradient_block, rows_own, (((1,), (1,)), ((), ())), preferred_element_type=jnp.float32
        ),
        lambda: lax.dot_general(
            gradient_block, cols_own, (((0,), (0,)), ((), ())), preferred_element_type=jnp.float32
        ),
    )
    stat_half = 0.9 * statistics[0] + 0.1 * gram_half
    eye_full = jnp.eye(block_order, dtype=jnp.float32)
    squares = jnp.sum(stat_half * stat_half)
    other_stat, other_squares = partner((stat_half, squares))
    frobenius = jnp.sqrt(squares + other_squares + 1e-06)
    root_scale = frobenius ** (-0.25)
    iterate_half = stat_half / frobenius
    full_iterate = assemble(stat_half, other_stat, half_index) / frobenius
    root_half = iterate_half
    for newton_step in range(NEWTON_MAX):
        if newton_step > 0:
            full_iterate = assemble(iterate_half, partner(iterate_half), half_index)
        tangent = (5.0 * eye_full - full_iterate) * 0.25
        if newton_step == 0:
            root_half = root_scale * column_half(tangent, half_index, half_width)
        else:
            advanced_root = product(tangent, root_half)
            root_half = jnp.where(newton_step < newton_count, advanced_root, root_half)
        if newton_step + 1 < NEWTON_MAX:
            square_half = product(tangent, column_half(tangent, half_index, half_width))
            square_full = assemble(square_half, partner(square_half), half_index)
            iterate_half = product(square_full, product(square_full, iterate_half))
    other_root = partner(root_half)
    block_float = gradient_block.astype(jnp.float32)
    payload = lax.cond(
        side_index == 0,
        lambda: lax.dot_general(
            root_half,
            block_float,
            (((0,), (0,)), ((), ())),
            precision=highest,
            preferred_element_type=jnp.float32,
        ),
        lambda: root_half.T,
    )
    received = opposite(payload)
    quarter = lax.cond(
        side_index == 0,
        lambda: lax.dot_general(
            payload,
            received,
            (((1,), (1,)), ((), ())),
            precision=highest,
            preferred_element_type=jnp.float32,
        ),
        lambda: product(received, other_root),
    )
    column_index = jnp.where(side_index == 0, half_index, 1 - half_index)
    grad_quarter = lax.dynamic_slice(
        block_float, (half_index * half_width, column_index * half_width), (half_width, half_width)
    )
    fresh_moment = 0.95 * moment[0] + 0.05 * grad_quarter * grad_quarter
    adam_step = grad_quarter / (jnp.sqrt(fresh_moment) + 1e-08)
    partial_sums = (jnp.sum(adam_step * adam_step), jnp.sum(quarter * quarter))
    pair_sums = partner(partial_sums)
    pair_total = (partial_sums[0] + pair_sums[0], partial_sums[1] + pair_sums[1])
    side_sums = opposite(pair_total)
    total_adam = pair_total[0] + side_sums[0]
    total_shaped = pair_total[1] + side_sums[1]
    entries = block_order * block_order
    graft_scale = jnp.sqrt(total_adam / entries) / jnp.sqrt(total_shaped / entries + 1e-12)
    direction = (graft_scale * quarter).astype(jnp.bfloat16)
    gathered = lax.all_gather(direction[None, None], "replica", axis=0, tiled=True)
    return (gathered, stat_half[None], fresh_moment[None])


def solution(mesh):
    placed = (
        P("replica", "fsdp", None),
        P(("replica", "fsdp"), None, None),
        P(("replica", "fsdp"), None, None),
        P("replica"),
        P("replica"),
    )
    return jax.shard_map(
        on_device,
        mesh=mesh,
        in_specs=placed,
        out_specs=(
            P(None, "fsdp", None, None),
            P(("replica", "fsdp"), None, None),
            P(("replica", "fsdp"), None, None),
        ),
        check_vma=False,
    )
```

profile of v0, /device:TPU:2, one launch (start us, length us, event | category | flops | bytes accessed | tf_op | source)
XLA Modules:
  0.0 315.9 jit_solution(14090443036180826345)
XLA Ops:
  10.3 16.8 %all-to-all-start = ((bf16[32,16,512]{2,1,0:T(8,128)(2,1)}), bf16[32,16,512]{2,1,0:T(8,128)(2,1)S(1)}, u32[]{:S(2)}, u32[]{:S(2)}) async-start(bf16[32,16,512]{2,1,0:T(8,128)(2,1)} %broadcast_select_fusion), calls=%async_computation | async-start | bytes 1048576 | tf_op jit(solution)/shard_map/all_to_all | solution.py:56
  31.0 10.2 %all-to-all-done = bf16[32,16,512]{2,1,0:T(8,128)(2,1)S(1)} async-done(((bf16[32,16,512]{2,1,0:T(8,128)(2,1)}), bf16[32,16,512]{2,1,0:T(8,128)(2,1)S(1)}, u32[]{:S(2)}, u32[]{:S(2)}) %all-to-all-start) | async-done | bytes 524320 | tf_op jit(solution)/shard_map/all_to_all | solution.py:56
  42.8 3.7 %collective-permute-start.2 = (f32[512,256]{0,1:T(8,128)S(1)}, f32[512,256]{0,1:T(8,128)S(1)}, u32[]{:S(2)}, u32[]{:S(2)}) collective-permute-start(f32[512,256]{0,1:T(8,128)S(1)} %get-tuple-element.85), channel_id=1, source_target_pairs={{0,1},{1,0},{2,3},{3,2},{4,5},{5,4},{6,7},{7,6},{8,9},{9,8},{10,11... | collective-permute-start | bytes 1572872 | tf_op jit(solution)/shard_map/ppermute | solution.py:19
  46.5 1.9 collective-permute-start.3
  52.5 2.1 collective-permute-start.4
  54.6 1.7 collective-permute-done.4
  56.4 1.8 fusion.14
  59.3 2.1 collective-permute-start.5
  61.5 1.7 collective-permute-done.5
  64.5 2.1 collective-permute-start.6
  66.6 1.7 collective-permute-done.6
  68.4 1.8 fusion.12
  70.2 1.9 fusion.11
  72.1 2.3 collective-permute-start.7
  76.4 2.2 convolution_select_fusion.1
  82.3 1.9 collective-permute-start.8
  84.3 2.2 collective-permute-start.9
  86.5 1.4 fusion.28
  88.0 2.1 collective-permute-start
  92.4 5.1 %collective-permute-start.1 = (f32[]{:T(128)}, f32[]{:T(128)}, u32[]{:S(2)}, u32[]{:S(2)}) collective-permute-start(f32[]{:T(128)} %add.96), channel_id=1, source_target_pairs={{0,2},{2,0},{1,3},{3,1},{4,6},{6,4},{5,7},{7,5},{8,10},{10,8},{9,1... | collective-permute-start | bytes 20 | tf_op jit(solution)/shard_map/ppermute | solution.py:19
  100.4 1.9 collective-permute-start.10
  104.9 5.6 %collective-permute-start.11 = (f32[]{:T(128)}, f32[]{:T(128)}, u32[]{:S(2)}, u32[]{:S(2)}) collective-permute-start(f32[]{:T(128)} %add.102), channel_id=1, source_target_pairs={{0,2},{2,0},{1,3},{3,1},{4,6},{6,4},{5,7},{7,5},{8,10},{10,8},{9,1... | collective-permute-start | bytes 20 | tf_op jit(solution)/shard_map/ppermute | solution.py:19
  113.2 191.2 %all-gather.3.cloned.1.call-done = bf16[8192,256]{1,0:T(8,128)(2,1)} async-done(((bf16[256,256]{1,0:T(8,128)(2,1)}), bf16[8192,256]{1,0:T(8,128)(2,1)}) %all-gather.3.cloned.1.call-update) | async-done | bytes 4194320 | tf_op jit(solution)/shard_map/all_gather | solution.py:137
  304.4 4.6 %copy.35 = bf16[32,1,256,256]{3,2,1,0:T(8,128)(2,1)} copy(bf16[32,1,256,256]{3,2,1,0:T(8,128)(2,1)} %bitcast.41) | data formatting | bytes 8388608
  (52 shorter events, 24.6 us)
Async XLA Ops:
  7.2 1.6 copy-start
  10.3 31.0 %all-to-all-start = ((bf16[32,16,512]{2,1,0:T(8,128)(2,1)}), bf16[32,16,512]{2,1,0:T(8,128)(2,1)S(1)}, u32[]{:S(2)}, u32[]{:S(2)}) async-start(bf16[32,16,512]{2,1,0:T(8,128)(2,1)} %broadcast_select_fusion), calls=%async_computation | async-start | bytes 1048576 | tf_op jit(solution)/shard_map/all_to_all | solution.py:56
  27.1 277.3 %all-gather.3.cloned.1.call-start = ((), (), s32[]{:S(2)}) async-start(), calls=%async_computation.1 | async-start | bytes 4325376 | tf_op jit(solution)/shard_map/all_gather | solution.py:137
  42.8 8.3 %collective-permute-start.2 = (f32[512,256]{0,1:T(8,128)S(1)}, f32[512,256]{0,1:T(8,128)S(1)}, u32[]{:S(2)}, u32[]{:S(2)}) collective-permute-start(f32[512,256]{0,1:T(8,128)S(1)} %get-tuple-element.85), channel_id=1, source_target_pairs={{0,1},{1,0},{2,3},{3,2},{4,5},{5,4},{6,7},{7,6},{8,9},{9,8},{10,11... | collective-permute-start | bytes 1572872 | tf_op jit(solution)/shard_map/ppermute | solution.py:19
  46.5 3.3 %collective-permute-start.3 = (f32[]{:T(128)}, f32[]{:T(128)}, u32[]{:S(2)}, u32[]{:S(2)}) collective-permute-start(f32[]{:T(128)} %get-tuple-element.84), channel_id=1, source_target_pairs={{0,1},{1,0},{2,3},{3,2},{4,5},{5,4},{6,7},{7,6},{8,9},{9,8},{10,11... | collective-permute-start | bytes 20 | tf_op jit(solution)/shard_map/ppermute | solution.py:19
  52.5 3.8 %collective-permute-start.4 = (f32[512,256]{0,1:T(8,128)S(1)}, f32[512,256]{0,1:T(8,128)S(1)}, u32[]{:S(2)}, u32[]{:S(2)}) collective-permute-start(f32[512,256]{0,1:T(8,128)S(1)} %fusion.23), channel_id=1, source_target_pairs={{0,1},{1,0},{2,3},{3,2},{4,5},{5,4},{6,7},{7,6},{8,9},{9,8},{10,11... | collective-permute-start | bytes 1572872 | tf_op jit(solution)/shard_map/ppermute | solution.py:19
  59.3 3.8 %collective-permute-start.5 = (f32[512,256]{0,1:T(8,128)S(1)}, f32[512,256]{0,1:T(8,128)S(1)}, u32[]{:S(2)}, u32[]{:S(2)}) collective-permute-start(f32[512,256]{0,1:T(8,128)S(1)} %fusion.13), channel_id=1, source_target_pairs={{0,1},{1,0},{2,3},{3,2},{4,5},{5,4},{6,7},{7,6},{8,9},{9,8},{10,11... | collective-permute-start | bytes 1572872 | tf_op jit(solution)/shard_map/ppermute | solution.py:19
  63.3 8.9 %copy-start.1 = (f32[512,256]{0,1:T(8,128)}, f32[512,256]{0,1:T(8,128)S(1)}, u32[]{:S(2)}) copy-start(f32[512,256]{0,1:T(8,128)S(1)} %get-tuple-element.97) | copy-start | bytes 1572868
  63.4 11.0 %copy-start.3 = (s32[8]{0:T(128)S(1)}, s32[8]{0:T(128)}, u32[]{:S(2)}) copy-start(s32[8]{0:T(128)} %param.15) | copy-start | bytes 100
  64.5 3.8 %collective-permute-start.6 = (f32[512,256]{0,1:T(8,128)S(1)}, f32[512,256]{0,1:T(8,128)S(1)}, u32[]{:S(2)}, u32[]{:S(2)}) collective-permute-start(f32[512,256]{0,1:T(8,128)S(1)} %fusion.16), channel_id=1, source_target_pairs={{0,1},{1,0},{2,3},{3,2},{4,5},{5,4},{6,7},{7,6},{8,9},{9,8},{10,11... | collective-permute-start | bytes 1572872 | tf_op jit(solution)/shard_map/ppermute | solution.py:19
  72.1 6.6 %collective-permute-start.7 = (f32[512,256]{0,1:T(8,128)}, f32[512,256]{0,1:T(8,128)}, u32[]{:S(2)}, u32[]{:S(2)}) collective-permute-start(f32[512,256]{0,1:T(8,128)} %fusion.11), channel_id=1, source_target_pairs={{0,1},{1,0},{2,3},{3,2},{4,5},{5,4},{6,7},{7,6},{8,9},{9,8},{10,11... | collective-permute-start | bytes 1572872 | tf_op jit(solution)/shard_map/ppermute | solution.py:19
  78.7 7.8 %copy-start.2 = (f32[1,256,256]{2,1,0:T(8,128)S(1)}, f32[1,256,256]{2,1,0:T(8,128)}, u32[]{:S(2)}) copy-start(f32[1,256,256]{2,1,0:T(8,128)} %param.13) | copy-start | bytes 786436
  82.3 16.8 %collective-permute-start.8 = (f32[256,512]{1,0:T(8,128)S(1)}, f32[256,512]{1,0:T(8,128)S(1)}, u32[]{:S(2)}, u32[]{:S(2)}) collective-permute-start(f32[256,512]{1,0:T(8,128)S(1)} %get-tuple-element.115), channel_id=1, source_target_pairs={{0,2},{2,0},{1,3},{3,1},{4,6},{6,4},{5,7},{7,5},{8,10},{10,8},{9,1... | collective-permute-start | bytes 1572872 | tf_op jit(solution)/shard_map/ppermute | solution.py:19
  84.3 14.9 %collective-permute-start.9 = (f32[512,256]{0,1:T(8,128)S(1)}, f32[512,256]{0,1:T(8,128)}, u32[]{:S(2)}, u32[]{:S(2)}) collective-permute-start(f32[512,256]{0,1:T(8,128)S(1)} %convolution_select_fusion), channel_id=1, source_target_pairs={{0,1},{1,0},{2,3},{3,2},{4,5},{5,4},{6,7},{7,6},{8,9},{9,8},{10,11... | collective-permute-start | bytes 1572872 | tf_op jit(solution)/shard_map/ppermute | solution.py:19
  88.0 3.1 collective-permute-start
  92.4 6.0 %collective-permute-start.1 = (f32[]{:T(128)}, f32[]{:T(128)}, u32[]{:S(2)}, u32[]{:S(2)}) collective-permute-start(f32[]{:T(128)} %add.96), channel_id=1, source_target_pairs={{0,2},{2,0},{1,3},{3,1},{4,6},{6,4},{5,7},{7,5},{8,10},{10,8},{9,1... | collective-permute-start | bytes 20 | tf_op jit(solution)/shard_map/ppermute | solution.py:19
  100.4 3.3 %collective-permute-start.10 = (f32[]{:T(128)}, f32[]{:T(128)}, u32[]{:S(2)}, u32[]{:S(2)}) collective-permute-start(f32[]{:T(128)} %get-tuple-element.81), channel_id=1, source_target_pairs={{0,1},{1,0},{2,3},{3,2},{4,5},{5,4},{6,7},{7,6},{8,9},{9,8},{10,11... | collective-permute-start | bytes 20 | tf_op jit(solution)/shard_map/ppermute | solution.py:19
  104.9 5.9 %collective-permute-start.11 = (f32[]{:T(128)}, f32[]{:T(128)}, u32[]{:S(2)}, u32[]{:S(2)}) collective-permute-start(f32[]{:T(128)} %add.102), channel_id=1, source_target_pairs={{0,2},{2,0},{1,3},{3,1},{4,6},{6,4},{5,7},{7,5},{8,10},{10,8},{9,1... | collective-permute-start | bytes 20 | tf_op jit(solution)/shard_map/ppermute | solution.py:19
Sparse Core Ops, SparseCore 0:
  112.3 192.0 all-gather.2
where the time goes:
time: 317 us; the launch traced here: 316 us
  waiting for transfers between devices  211 us (67%)
  starting transfers between devices  49.9 us (16%)
  between operations  23.7 us (7%)
  matrix products  14.8 us (5%)
  other arithmetic  7.98 us (3%)
  local copies, waits for them, and re-layouts  7.92 us (2%)
    all_gather x1, waiting for transfers between devices, on_device(): lax.all_gather(direction[None, None], 'replica', axis=0, tiled=True)  191 us
    ppermute x12, starting transfers between devices, partner_2(): return lax.ppermute(block, axis, route)  33.1 us
    all_to_all x1, starting transfers between devices, on_device(): lax.all_to_all(outgoing, 'fsdp', split_axis=0, concat_axis=0, tiled=True)  16.8 us
    dot_general x8, matrix products, product(): jnp.dot(left_part, right_part, precision=highest, preferred_element_type=...  12.2 us
    all_to_all x1, waiting for transfers between devices, on_device(): lax.all_to_all(outgoing, 'fsdp', split_axis=0, concat_axis=0, tiled=True)  10.2 us
    ppermute x12, waiting for transfers between devices, partner_2(): return lax.ppermute(block, axis, route)  9.95 us
    unnamed x11, local copies, waits for them, and re-layouts  6.9 us
  transfers between devices with their start and end apart: 14, of which 10 were waited for; matrix products, arithmetic and copies ran while one was open for 2% of the time, Pallas kernels for 0%

commit v1 on v0

v1 whole, which is shorter than its diff:
```python
import functools

import jax
import jax.numpy as jnp
from jax import lax
from jax.experimental import pallas as pl
from jax.experimental.pallas import tpu as pltpu
from jax.sharding import PartitionSpec as P

MESH = pl.DeviceIdType.MESH


def make_plan(cross, chunks, tz=2.95, ty=6.2, lz=1.6, ly=2.6):
    routes = {}
    def add(a, s, b): routes.setdefault(a, []).append((s, b))
    def norm(d): return d if d <= 8 else d - 16
    half = chunks // 2
    for c in range(chunks):
        for d in range(0, 7): add((0, d, c), '+', (0, d + 1, c))
        for d in range(0, -7, -1): add((0, d, c), '-', (0, d - 1, c))
        if c < half: add((0, 7, c), '+', (0, 8, c))
        else: add((0, -7, c), '-', (0, 8, c))
        for d in cross: add((0, d, c), 'y', (1, d, c))
        cs = sorted(x % 16 for x in cross)
        flip = 0
        for i, a in enumerate(cs):
            b = cs[(i + 1) % len(cs)]
            if b <= a: b += 16
            n = b - a - 1
            left = n // 2; right = n // 2
            if n % 2:
                if (c < half) : left += 1
                else: right += 1
            for j in range(left): add((1, norm((a + j) % 16), c), '+', (1, norm((a + j + 1) % 16), c))
            for j in range(right): add((1, norm((b - j) % 16), c), '-', (1, norm((b - j - 1) % 16), c))
    import functools
    cost = {'+': tz / chunks + lz, '-': tz / chunks + lz, 'y': ty / chunks + ly}
    @functools.lru_cache(None)
    def rem(item):
        return max([cost[s] + rem(b) for s, b in routes.get(item, [])], default=0)
    dur = {'+': tz / chunks, '-': tz / chunks, 'y': ty / chunks}
    lat = {'+': lz, '-': lz, 'y': ly}
    free = {'+': 0., '-': 0., 'y': 0.}
    ready = {'+': [], '-': [], 'y': []}
    def arrive(item, t):
        for s, b in routes.get(item, []):
            ready[s].append((t, item, b))
    for c in range(chunks): arrive((0, 0, c), 0.0)
    order = []; end = 0
    while any(ready.values()):
        best = None
        for s in ready:
            if not ready[s]: continue
            t = max(free[s], min(r[0] for r in ready[s]))
            if best is None or t < best[0]: best = (t, s)
        t, s = best
        cand = [r for r in ready[s] if r[0] <= t + 1e-9]
        cand.sort(key=lambda r: (-(cost[s] + rem(r[2])), r[0], r[1]))
        r = cand[0]; ready[s].remove(r)
        free[s] = t + dur[s]
        order.append((t, s, r[1], r[2]))
        ta = t + dur[s] + lat[s]
        end = max(end, ta)
        arrive(r[2], ta)
    recvd = {}
    for t, s, a, b in order:
        assert b not in recvd, b
        recvd[b] = 1
    assert len(recvd) == 31 * chunks, len(recvd)
    nz = {s: sum(1 for o in order if o[1] == s) / chunks for s in '+-y'}
    return order, end, nz


def split(value):
    high = value.astype(jnp.bfloat16)
    return high, (value - high.astype(jnp.float32)).astype(jnp.bfloat16)


def dot(left, right):
    return jnp.dot(left, right, preferred_element_type=jnp.float32)


def dot_nt(left, right):
    return lax.dot_general(left, right, (((1,), (1,)), ((), ())), preferred_element_type=jnp.float32)


def dot_3(left_high, left_low, right_high, right_low):
    return dot(left_high, right_high) + (dot(left_high, right_low) + dot(left_low, right_high))


def shifted(rows, first_row, width):
    row = lax.broadcasted_iota(jnp.int32, rows.shape, 0) + first_row
    column = lax.broadcasted_iota(jnp.int32, rows.shape, 1)
    return jnp.where(row == column, 1.25, 0.0) - 0.25 * rows


def step_kernel(
    order,
    chunks,
    assign_hbm,
    newton_hbm,
    grad_hbm,
    stat_ref,
    moment_hbm,
    dir_ref,
    new_stat_ref,
    new_moment_ref,
    assign_ref,
    newton_ref,
    grad_ref,
    own_half,
    moment_ref,
    outgoing,
    block,
    block_turned,
    old,
    factor,
    core_grad,
    t_high,
    t_low,
    m_high,
    m_low,
    s_high,
    s_low,
    u_high,
    u_low,
    sent_root,
    other_root,
    quarter_ref,
    sums,
    own_direction,
    input_sem,
    output_sem,
    grad_send,
    grad_recv,
    pass_send,
    pass_recv,
    old_send,
    old_pass,
    old_recv,
    old_local,
    root_send,
    root_recv,
    sum_send,
    sum_recv,
    dir_send,
    dir_recv,
    dir_local,
):
    replica, fsdp = lax.axis_index("replica"), lax.axis_index("fsdp")
    z, y_high = replica // 2, lax.rem(replica, 2)
    chip, core = fsdp // 2, lax.rem(fsdp, 2)
    slot, side = chip // 2, lax.rem(chip, 2)
    member = lax.rem(fsdp, 4)
    twin = (replica, chip * 2 + 1 - core)
    beside = (replica, slot * 4 + (1 - side) * 2 + side)
    upward = (lax.rem(z + 1, 16) * 2 + y_high, fsdp)
    downward = (lax.rem(z + 15, 16) * 2 + y_high, fsdp)
    across = (z * 2 + 1 - y_high, fsdp)

    def same_core(distance):
        return (replica, lax.rem(chip + distance, 16) * 2 + core)

    def remote(source, target, send_sem, recv_sem, device):
        return pltpu.make_async_remote_copy(
            src_ref=source,
            dst_ref=target,
            send_sem=send_sem,
            recv_sem=recv_sem,
            device_id=device,
            device_id_type=MESH,
        )

    pairs = (
        (assign_hbm, assign_ref),
        (grad_hbm, grad_ref),
        (newton_hbm, newton_ref),
        (stat_ref.at[0], own_half),
        (moment_hbm.at[0], moment_ref),
    )
    inputs = [pltpu.make_async_copy(source, target, input_sem.at[i]) for i, (source, target) in enumerate(pairs)]
    for copy in inputs:
        copy.start()
    barrier = pltpu.get_barrier_semaphore()
    diagonal = (replica, slot * 4 + (1 - side) * 2 + (1 - core))
    greeted = [same_core(distance) for distance in range(1, 16)] + [twin, diagonal, upward, downward, across]
    for device in greeted:
        pl.semaphore_signal(barrier, inc=1, device_id=device, device_id_type=MESH)
    inputs[0].wait()
    inputs[1].wait()
    for target_slot in range(8):
        outgoing[target_slot] = grad_ref[lax.rem(assign_ref[target_slot], 8)]
    block[chip, core] = outgoing[slot]
    pl.semaphore_wait(barrier, len(greeted))

    grad_copies = []
    for distance in range(1, 16):
        target = lax.rem(chip + distance, 16)
        copy = remote(
            outgoing.at[target // 2],
            block.at[chip, core],
            grad_send.at[distance],
            grad_recv.at[distance],
            same_core(distance),
        )
        copy.start()
        grad_copies.append(copy)

    def old_piece(number):
        half, first = ((0, 0), (0, 256), (1, 256))[number]
        source = stat_ref.at[0, pl.ds(first, 256), :]
        here = old.at[number]
        return (
            half,
            remote(source, here, old_send.at[number], old_recv.at[number], beside),
            remote(source, here, old_pass.at[number], old_recv.at[number], twin),
            pltpu.make_async_copy(source, here, old_local.at[number]),
        )

    for number in range(3):
        half, to_beside, to_twin, to_self = old_piece(number)

        @pl.when(core == half)
        def _():
            to_beside.start()

        @pl.when((core == half) & (core == side))
        def _():
            to_self.start()

        @pl.when((core == half) & (core != side))
        def _():
            to_twin.start()

    pass_copies = []
    for distance in range(16):
        source = lax.rem(chip + 16 - distance, 16)
        if distance > 0:
            grad_copies[distance - 1].wait_recv()
        rows = block.at[source, core]
        copy = remote(rows, rows, pass_send.at[distance], pass_recv.at[distance], twin)
        copy.start()
        pass_copies.append(copy)
    for copy in pass_copies:
        copy.wait_recv()

    taken = assign_ref[slot]
    received = block[...].reshape(512, 512)
    row = lax.broadcasted_iota(jnp.int32, (512, 512), 0)
    column = lax.broadcasted_iota(jnp.int32, (512, 512), 1)
    identity = jnp.where(row == column, 1.0, 0.0).astype(jnp.bfloat16)
    flipped = dot_nt(identity, received)
    block_turned[...] = flipped.astype(jnp.bfloat16)

    def oriented(which):
        weight = lax.rem(taken // 8 + which, 2).astype(jnp.float32)
        plain = block[...].reshape(512, 512).astype(jnp.float32)
        return (plain * (1.0 - weight) + block_turned[...].astype(jnp.float32) * weight).astype(jnp.bfloat16)

    core_grad[...] = oriented(core)
    grams = [dot_nt(core_grad[pl.ds(part * 256, 256), :], core_grad[...]) for part in range(2)]
    for number in range(3):
        half, to_beside, to_twin, to_self = old_piece(number)
        local = (core == half) & (core == side)

        @pl.when(local)
        def _():
            to_self.wait()

        @pl.when(jnp.logical_not(local))
        def _():
            to_beside.wait_recv()

    lower = old[1]
    quarters = ((old[0], lower.T), (lower, old[2]))
    squares = jnp.zeros((1, 1), jnp.float32)
    for part in range(2):
        rows = pl.ds(part * 256, 256)
        for half in range(2):
            entry = 0.9 * quarters[part][half] + 0.1 * grams[part][:, half * 256 : (half + 1) * 256]
            factor[rows, pl.ds(half * 256, 256)] = entry
            squares = squares + jnp.sum(entry * entry, keepdims=True)
    norm = jnp.sqrt(squares + 1e-06)
    inverse = 1.0 / norm
    scale = lax.rsqrt(jnp.sqrt(norm))

    for part in range(2):
        rows = pl.ds(part * 256, 256)
        iterate = factor[rows, :] * inverse
        m_high[rows, :], m_low[rows, :] = split(iterate)
        tangent = shifted(iterate, part * 256, 512)
        factor[rows, :] = tangent
        t_high[rows, :], t_low[rows, :] = split(tangent)
    for part in range(2):
        rows = pl.ds(part * 256, 256)
        s_high[rows, :], s_low[rows, :] = split(dot_3(t_high[rows, :], t_low[rows, :], t_high[...], t_low[...]))
    for part in range(2):
        rows = pl.ds(part * 256, 256)
        u_high[rows, :], u_low[rows, :] = split(dot_3(s_high[rows, :], s_low[rows, :], m_high[...], m_low[...]))
    for part in range(2):
        rows = pl.ds(part * 256, 256)
        iterate = dot_3(s_high[rows, :], s_low[rows, :], u_high[...], u_low[...])
        m_high[rows, :], m_low[rows, :] = split(iterate)
        t_high[rows, :], t_low[rows, :] = split(shifted(iterate, part * 256, 512))

    for part in range(2):
        rows = pl.ds(part * 256, 256)
        s_high[rows, :], s_low[rows, :] = split(dot_3(t_high[rows, :], t_low[rows, :], t_high[...], t_low[...]))
    inputs[2].wait()
    steps = newton_ref[lax.rem(taken, 8)]

    def root_rows(first):
        start = factor[pl.ds(pl.multiple_of(first * 256, 256), 256), :]
        second = dot_3(*split(start), t_high[...], t_low[...])
        third = dot_3(*split(second), m_high[...], m_low[...])
        third = dot_3(*split(third), s_high[...], s_low[...])
        third = dot_3(*split(third), s_high[...], s_low[...])
        third = 1.25 * second - 0.25 * third
        return scale * jnp.where(jnp.full((256, 512), steps) > 2, third, second)

    own = core * (1 - side)
    sent_root[...] = root_rows(1 - own)
    root_copy = remote(sent_root, other_root, root_send, root_recv, twin)
    root_copy.start()
    root_high, root_low = split(root_rows(own))
    shaped = dot(root_high, core_grad[...]) + dot(root_low, core_grad[...])
    u_high[0:256, :], u_low[0:256, :] = split(shaped)

    first_row = pl.multiple_of(own * 256, 256)
    first_column = pl.multiple_of((side * (1 - core) + core) * 256, 256)
    quarter_ref[...] = core_grad[pl.ds(first_row, 256), pl.ds(first_column, 256)].astype(jnp.float32)

    @pl.when(core == 1)
    def _():
        quarter_ref[...] = quarter_ref[...].T

    inputs[4].wait()
    entries = quarter_ref[...]
    fresh = 0.95 * moment_ref[...] + 0.05 * entries * entries
    moment_ref[...] = fresh
    adam = entries / (jnp.sqrt(fresh) + 1e-08)
    adam_sum = jnp.sum(adam * adam, keepdims=True)
    moment_out = pltpu.make_async_copy(moment_ref, new_moment_ref.at[0], output_sem.at[0])
    moment_out.start()
    root_copy.wait_recv()
    root_high, root_low = split(other_root[...])
    shaped_high, shaped_low = u_high[0:256, :], u_low[0:256, :]
    quarter = dot_nt(shaped_high, root_high) + (dot_nt(shaped_high, root_low) + dot_nt(shaped_low, root_high))
    quarter_ref[...] = quarter
    quarter_sum = jnp.sum(quarter * quarter, keepdims=True)
    line = lax.broadcasted_iota(jnp.int32, (8, 128), 0)
    sums[member] = jnp.where(line == 0, adam_sum, quarter_sum)
    sum_copies = []
    for distance in range(1, 4):
        device = (replica, slot * 4 + lax.rem(member + distance, 4))
        copy = remote(sums.at[member], sums.at[member], sum_send.at[distance], sum_recv.at[distance], device)
        copy.start()
        sum_copies.append(copy)

    @pl.when(core == 1)
    def _():
        quarter_ref[...] = quarter_ref[...].T

    for copy in sum_copies:
        copy.wait_recv()
    total = (sums[0] + sums[1]) + (sums[2] + sums[3])
    mean = total * (1.0 / (512 * 512))
    graft = jnp.sqrt(mean[0:1, 0:1]) / jnp.sqrt(mean[1:2, 0:1] + 1e-12)
    own_direction[...] = (graft * quarter_ref[...]).astype(jnp.bfloat16)

    keep = pltpu.make_async_copy(own_direction, dir_ref.at[replica, 0], dir_local)
    keep.start()
    height = 256 // chunks
    numbers = {send[3]: number for number, send in enumerate(order)}
    ways = {"+": upward, "-": downward, "y": across}

    def place(item):
        kind, distance, chunk = item
        column_of = y_high if kind == 0 else 1 - y_high
        return dir_ref.at[lax.rem(z + 16 - distance, 16) * 2 + column_of, 0, pl.ds(chunk * height, height), :]

    arrived = {(0, 0, chunk) for chunk in range(chunks)}

    def await_item(item):
        if item not in arrived:
            arrived.add(item)
            remote(place(item), place(item), dir_send.at[0], dir_recv.at[numbers[item]], upward).wait_recv()

    dir_copies = []
    stat_out = pltpu.make_async_copy(own_half, new_stat_ref.at[0], output_sem.at[1])
    for number, (_, way, item, landing) in enumerate(order):
        if number == 3 * chunks:
            inputs[3].wait()
            block_turned[...] = oriented(side)
            half_rows = block_turned[pl.ds(pl.multiple_of(core * 256, 256), 256), :]
            own_half[...] = 0.9 * own_half[...] + 0.1 * dot_nt(block_turned[...], half_rows)
            stat_out.start()
        await_item(item)
        source = place(item)
        if item[:2] == (0, 0):
            source = own_direction.at[pl.ds(item[2] * height, height), :]
        copy = remote(source, place(item), dir_send.at[number], dir_recv.at[number], ways[way])
        copy.start()
        dir_copies.append(copy)
    for item in numbers:
        await_item(item)
    keep.wait()
    moment_out.wait()
    stat_out.wait()
    root_copy.wait_send()
    for number in range(3):
        half, to_beside, to_twin, to_self = old_piece(number)

        @pl.when(core == half)
        def _():
            to_beside.wait_send()

        @pl.when((core == half) & (core != side))
        def _():
            to_twin.wait_send()

    for copy in grad_copies + pass_copies + sum_copies + dir_copies:
        copy.wait_send()


CROSSINGS = (0, 3, 6, -6, -3)
CHUNKS = 2


def on_device(grad, statistics, moment, assignment, newton_steps):
    order = make_plan(CROSSINGS, CHUNKS)[0]
    anywhere = pl.BlockSpec(memory_space=pl.ANY)
    wide_16 = pltpu.VMEM((512, 512), jnp.bfloat16)
    wide_32 = pltpu.VMEM((512, 512), jnp.float32)
    dma = pltpu.SemaphoreType.DMA
    return pl.pallas_call(
        functools.partial(step_kernel, order, CHUNKS),
        out_shape=(
            jax.ShapeDtypeStruct((32, 1, 256, 256), jnp.bfloat16),
            jax.ShapeDtypeStruct((1, 512, 256), jnp.float32),
            jax.ShapeDtypeStruct((1, 256, 256), jnp.float32),
        ),
        in_specs=[anywhere] * 5,
        out_specs=(anywhere, anywhere, anywhere),
        scratch_shapes=[
            pltpu.SMEM((8,), jnp.int32),
            pltpu.SMEM((8,), jnp.int32),
            pltpu.VMEM((8, 16, 512), jnp.bfloat16),
            pltpu.VMEM((512, 256), jnp.float32),
            pltpu.VMEM((256, 256), jnp.float32),
            pltpu.VMEM((8, 16, 512), jnp.bfloat16),
            pltpu.VMEM((16, 2, 16, 512), jnp.bfloat16),
            wide_16,
            pltpu.VMEM((3, 256, 256), jnp.float32),
            wide_32,
        ]
        + [wide_16] * 9
        + [
            pltpu.VMEM((256, 512), jnp.float32),
            pltpu.VMEM((256, 512), jnp.float32),
            pltpu.VMEM((256, 256), jnp.float32),
            pltpu.VMEM((4, 8, 128), jnp.float32),
            pltpu.VMEM((256, 256), jnp.bfloat16),
            dma((5,)),
            dma((2,)),
            dma((16,)),
            dma((16,)),
            dma((16,)),
            dma((16,)),
            dma((3,)),
            dma((3,)),
            dma((3,)),
            dma((3,)),
            dma,
            dma,
            dma((4,)),
            dma((4,)),
            dma((len(order),)),
            dma((len(order),)),
            dma,
        ],
        compiler_params=pltpu.CompilerParams(
            collective_id=0, has_side_effects=True, vmem_limit_bytes=60 << 20
        ),
        name="shampoo_step",
    )(assignment, newton_steps, grad, statistics, moment)


def solution(mesh):
    placed = (
        P("replica", "fsdp", None),
        P(("replica", "fsdp"), None, None),
        P(("replica", "fsdp"), None, None),
        P("replica"),
        P("replica"),
    )
    return jax.shard_map(
        on_device,
        mesh=mesh,
        in_specs=placed,
        out_specs=(
            P(None, "fsdp", None, None),
            P(("replica", "fsdp"), None, None),
            P(("replica", "fsdp"), None, None),
        ),
        check_vma=False,
    )
```

time: 317 us -> 102 us (0.32)
  the two profiles are of different devices: /device:TPU:2 before, /device:TPU:24 now
where the time goes in v1:
time: 102 us
  Pallas kernels  94.8 us (93%)
  local copies, waits for them, and re-layouts  6.21 us (6%)
    pallas_call x1, Pallas kernels, on_device(): pl.pallas_call(functools.partial(step_kernel, order, CHUNKS), out_shape=(...  94.8 us
    unnamed x7, local copies, waits for them, and re-layouts  6.21 us

profile of v1, /device:TPU:24, one launch (start us, length us, event | category | flops | bytes accessed | tf_op | source)
XLA Modules:
  0.0 101.6 jit_solution(10018877920606167468)
XLA Ops:
  0.6 94.8 %shampoo_step.1 = (bf16[32,1,256,256]{3,2,1,0:T(8,128)(2,1)}, f32[1,512,256]{2,1,0:T(8,128)}, f32[1,256,256]{2,1,0:T(8,128)}) custom-call(s32[8]{0:T(128)} %assign_hbm.1, s32[8]{0:T(128)} %newton_hbm.1, bf16[8,16,512]{2,1,0:T(8,128)(2,1)} %grad_hbm.1, f32[1,512,256]{2,1,0:T(8,128)} %stat_ref.1, f32[1,256,256]{2,1,0:T(8,128)} %moment_hbm.1), custom_call_target="tpu_custom_call" | custom-call | tf_op jit(solution)/shard_map/shampoo_step/pallas_call | solution.py:436
  95.4 0.0 copy-start
  95.4 0.0 copy-start.1
  95.4 4.7 %copy.11 = bf16[32,1,256,256]{3,2,1,0:T(8,128)(2,1)} copy(bf16[32,1,256,256]{3,2,1,0:T(8,128)(2,1)} %get-tuple-element.6) | data formatting | bytes 8388608
  100.1 0.0 copy-done
  100.1 0.8 copy.12
  100.9 0.0 copy-done.1
  100.9 0.7 copy.13
Async XLA Ops:
  95.4 4.7 %copy-start = (f32[1,512,256]{2,1,0:T(8,128)S(1)}, f32[1,512,256]{2,1,0:T(8,128)}, u32[]{:S(2)}) copy-start(f32[1,512,256]{2,1,0:T(8,128)} %get-tuple-element.7) | copy-start | bytes 1572868
  95.4 5.5 %copy-start.1 = (f32[1,256,256]{2,1,0:T(8,128)S(1)}, f32[1,256,256]{2,1,0:T(8,128)}, u32[]{:S(2)}) copy-start(f32[1,256,256]{2,1,0:T(8,128)} %get-tuple-element.8) | copy-start | bytes 786436

commit v2 on v1

--- a/solution.py
+++ b/solution.py
@@ -427,13 +427,26 @@
 CHUNKS = 2
 
 
+def place_kernel(dir_ref, stat_ref, moment_ref, dir_out, stat_out, moment_out, sem):
+    copies = [
+        pltpu.make_async_copy(dir_ref.at[pl.ds(part * 8, 8)], dir_out.at[pl.ds(part * 8, 8)], sem.at[part])
+        for part in range(4)
+    ]
+    copies.append(pltpu.make_async_copy(stat_ref, stat_out, sem.at[4]))
+    copies.append(pltpu.make_async_copy(moment_ref, moment_out, sem.at[5]))
+    for copy in copies:
+        copy.start()
+    for copy in copies:
+        copy.wait()
+
+
 def on_device(grad, statistics, moment, assignment, newton_steps):
     order = make_plan(CROSSINGS, CHUNKS)[0]
     anywhere = pl.BlockSpec(memory_space=pl.ANY)
     wide_16 = pltpu.VMEM((512, 512), jnp.bfloat16)
     wide_32 = pltpu.VMEM((512, 512), jnp.float32)
     dma = pltpu.SemaphoreType.DMA
-    return pl.pallas_call(
+    results = pl.pallas_call(
         functools.partial(step_kernel, order, CHUNKS),
         out_shape=(
             jax.ShapeDtypeStruct((32, 1, 256, 256), jnp.bfloat16),
@@ -480,10 +493,19 @@
             dma,
         ],
         compiler_params=pltpu.CompilerParams(
-            collective_id=0, has_side_effects=True, vmem_limit_bytes=60 << 20
+            collective_id=0, has_side_effects=True, vmem_limit_bytes=24 << 20
         ),
         name="shampoo_step",
-    )(assignment, newton_steps, grad, statistics, moment)
+    )(*(pltpu.with_memory_space_constraint(x, pltpu.HBM) for x in (assignment, newton_steps, grad, statistics, moment)))
+    return pl.pallas_call(
+        place_kernel,
+        out_shape=tuple(jax.ShapeDtypeStruct(result.shape, result.dtype) for result in results),
+        in_specs=[anywhere] * 3,
+        out_specs=[anywhere] * 3,
+        scratch_shapes=[dma((6,))],
+        compiler_params=pltpu.CompilerParams(vmem_limit_bytes=8 << 20),
+        name="place_results",
+    )(*results)
 
 
 def solution(mesh):

time: 102 us -> 97.1 us (0.952)
  the two profiles are of different devices: /device:TPU:24 before, /device:TPU:2 now
where the time goes in v2:
time: 97.1 us; the launch traced here: 96.9 us
  Pallas kernels  96.3 us (99%)
    pallas_call x1, Pallas kernels, on_device(): pl.pallas_call(functools.partial(step_kernel, order, CHUNKS), out_shape=(...  94 us
    pallas_call x1, Pallas kernels, on_device(): pl.pallas_call(place_kernel, out_shape=tuple((jax.ShapeDtypeStruct(result...  2.3 us

profile of v2, /device:TPU:2, one launch (start us, length us, event | category | flops | bytes accessed | tf_op | source)
XLA Modules:
  0.0 96.9 jit_solution(17792138831605191742)
XLA Ops:
  0.6 94.0 %shampoo_step.1 = (bf16[32,1,256,256]{3,2,1,0:T(8,128)(2,1)S(1)}, f32[1,512,256]{2,1,0:T(8,128)S(1)}, f32[1,256,256]{2,1,0:T(8,128)S(1)}) custom-call(s32[8]{0:T(128)} %assign_hbm.1, s32[8]{0:T(128)} %newton_hbm.1, bf16[8,16,512]{2,1,0:T(8,128)(2,1)} %grad_hbm.1, f32[1,512,256]{2,1,0:T(8,128)} %stat_ref.1, f32[1,256,256]{2,1,0:T(8,128)} %moment_hbm.1), custom_call_target="tpu_custom_call" | custom-call | tf_op jit(solution)/shard_map/shampoo_step/pallas_call | solution.py:449
  94.6 2.3 %place_results.1 = (bf16[32,1,256,256]{3,2,1,0:T(8,128)(2,1)}, f32[1,512,256]{2,1,0:T(8,128)}, f32[1,256,256]{2,1,0:T(8,128)}) custom-call(bf16[32,1,256,256]{3,2,1,0:T(8,128)(2,1)S(1)} %get-tuple-element.6.dir_ref, f32[1,512,256]{2,1,0:T(8,128)S(1)} %get-tuple-element.7.stat_ref, f32[1,256,256]{2,1,0:T(8,128)S(1)} %get-tuple-element.8.moment_ref), custom_call_target="tpu_custom_call" | custom-call | tf_op jit(solution)/shard_map/place_results/pallas_call | solution.py:500

commit v3 on v2

--- a/solution.py
+++ b/solution.py
@@ -207,9 +207,9 @@
         grad_copies.append(copy)
 
     def old_piece(number):
-        half, first = ((0, 0), (0, 256), (1, 256))[number]
-        source = stat_ref.at[0, pl.ds(first, 256), :]
-        here = old.at[number]
+        half, first, count, width, landing = OLD_PIECES[number]
+        source = stat_ref.at[0, pl.ds(first, count), pl.ds(0, width)]
+        here = old.at[pl.ds(landing, count), pl.ds(0, width)]
         return (
             half,
             remote(source, here, old_send.at[number], old_recv.at[number], beside),
@@ -217,7 +217,7 @@
             pltpu.make_async_copy(source, here, old_local.at[number]),
         )
 
-    for number in range(3):
+    for number in range(4):
         half, to_beside, to_twin, to_self = old_piece(number)
 
         @pl.when(core == half)
@@ -253,13 +253,12 @@
     block_turned[...] = flipped.astype(jnp.bfloat16)
 
     def oriented(which):
-        weight = lax.rem(taken // 8 + which, 2).astype(jnp.float32)
-        plain = block[...].reshape(512, 512).astype(jnp.float32)
-        return (plain * (1.0 - weight) + block_turned[...].astype(jnp.float32) * weight).astype(jnp.bfloat16)
+        plain = block[...].reshape(512, 512)
+        return jnp.where(lax.rem(taken // 8 + which, 2) == 1, block_turned[...], plain)
 
     core_grad[...] = oriented(core)
     grams = [dot_nt(core_grad[pl.ds(part * 256, 256), :], core_grad[...]) for part in range(2)]
-    for number in range(3):
+    for number in range(4):
         half, to_beside, to_twin, to_self = old_piece(number)
         local = (core == half) & (core == side)
 
@@ -271,8 +270,10 @@
         def _():
             to_beside.wait_recv()
 
-    lower = old[1]
-    quarters = ((old[0], lower.T), (lower, old[2]))
+    for first in (0, 512):
+        old[pl.ds(first, 128), pl.ds(128, 128)] = old[pl.ds(first + 128, 128), pl.ds(0, 128)].T
+    lower = old[256:512, :]
+    quarters = ((old[0:256, :], lower.T), (lower, old[512:768, :]))
     squares = jnp.zeros((1, 1), jnp.float32)
     for part in range(2):
         rows = pl.ds(part * 256, 256)
@@ -388,8 +389,10 @@
 
     dir_copies = []
     stat_out = pltpu.make_async_copy(own_half, new_stat_ref.at[0], output_sem.at[1])
+    placed = False
     for number, (_, way, item, landing) in enumerate(order):
-        if number == 3 * chunks:
+        if not placed and item not in arrived:
+            placed = True
             inputs[3].wait()
             block_turned[...] = oriented(side)
             half_rows = block_turned[pl.ds(pl.multiple_of(core * 256, 256), 256), :]
@@ -408,7 +411,7 @@
     moment_out.wait()
     stat_out.wait()
     root_copy.wait_send()
-    for number in range(3):
+    for number in range(4):
         half, to_beside, to_twin, to_self = old_piece(number)
 
         @pl.when(core == half)
@@ -423,6 +426,7 @@
         copy.wait_send()
 
 
+OLD_PIECES = ((0, 128, 384, 256, 128), (1, 384, 128, 256, 640), (0, 0, 128, 128, 0), (1, 256, 128, 128, 512))
 CROSSINGS = (0, 3, 6, -6, -3)
 CHUNKS = 2
 
@@ -464,7 +468,7 @@
             pltpu.VMEM((8, 16, 512), jnp.bfloat16),
             pltpu.VMEM((16, 2, 16, 512), jnp.bfloat16),
             wide_16,
-            pltpu.VMEM((3, 256, 256), jnp.float32),
+            pltpu.VMEM((768, 256), jnp.float32),
             wide_32,
         ]
         + [wide_16] * 9
@@ -480,10 +484,10 @@
             dma((16,)),
             dma((16,)),
             dma((16,)),
-            dma((3,)),
-            dma((3,)),
-            dma((3,)),
-            dma((3,)),
+            dma((4,)),
+            dma((4,)),
+            dma((4,)),
+            dma((4,)),
             dma,
             dma,
             dma((4,)),

time: 97.1 us -> 95.6 us (0.985)
  the two profiles are of different devices: /device:TPU:2 before, /device:TPU:16 now
where the time goes in v3:
time: 95.6 us; the launch traced here: 95.5 us
  Pallas kernels  94.8 us (99%)
    pallas_call x1, Pallas kernels, on_device(): pl.pallas_call(functools.partial(step_kernel, order, CHUNKS), out_shape=(...  92.5 us
    pallas_call x1, Pallas kernels, on_device(): pl.pallas_call(place_kernel, out_shape=tuple((jax.ShapeDtypeStruct(result...  2.3 us

profile of v3, /device:TPU:16, one launch (start us, length us, event | category | flops | bytes accessed | tf_op | source)
XLA Modules:
  0.0 95.5 jit_solution(3265605173294107973)
XLA Ops:
  0.6 92.5 %shampoo_step.1 = (bf16[32,1,256,256]{3,2,1,0:T(8,128)(2,1)S(1)}, f32[1,512,256]{2,1,0:T(8,128)S(1)}, f32[1,256,256]{2,1,0:T(8,128)S(1)}) custom-call(s32[8]{0:T(128)} %assign_hbm.1, s32[8]{0:T(128)} %newton_hbm.1, bf16[8,16,512]{2,1,0:T(8,128)(2,1)} %grad_hbm.1, f32[1,512,256]{2,1,0:T(8,128)} %stat_ref.1, f32[1,256,256]{2,1,0:T(8,128)} %moment_hbm.1), custom_call_target="tpu_custom_call" | custom-call | tf_op jit(solution)/shard_map/shampoo_step/pallas_call | solution.py:453
  93.2 2.3 %place_results.1 = (bf16[32,1,256,256]{3,2,1,0:T(8,128)(2,1)}, f32[1,512,256]{2,1,0:T(8,128)}, f32[1,256,256]{2,1,0:T(8,128)}) custom-call(bf16[32,1,256,256]{3,2,1,0:T(8,128)(2,1)S(1)} %get-tuple-element.6.dir_ref, f32[1,512,256]{2,1,0:T(8,128)S(1)} %get-tuple-element.7.stat_ref, f32[1,256,256]{2,1,0:T(8,128)S(1)} %get-tuple-element.8.moment_ref), custom_call_target="tpu_custom_call" | custom-call | tf_op jit(solution)/shard_map/place_results/pallas_call | solution.py:504

commit v4 on v3

--- a/solution.py
+++ b/solution.py
@@ -186,6 +186,9 @@
     greeted = [same_core(distance) for distance in range(1, 16)] + [twin, diagonal, upward, downward, across]
     for device in greeted:
         pl.semaphore_signal(barrier, inc=1, device_id=device, device_id_type=MESH)
+    row = lax.broadcasted_iota(jnp.int32, (512, 512), 0)
+    column = lax.broadcasted_iota(jnp.int32, (512, 512), 1)
+    t_high[...] = jnp.where(row == column, 1.0, 0.0).astype(jnp.bfloat16)
     inputs[0].wait()
     inputs[1].wait()
     for target_slot in range(8):
@@ -246,10 +249,7 @@
 
     taken = assign_ref[slot]
     received = block[...].reshape(512, 512)
-    row = lax.broadcasted_iota(jnp.int32, (512, 512), 0)
-    column = lax.broadcasted_iota(jnp.int32, (512, 512), 1)
-    identity = jnp.where(row == column, 1.0, 0.0).astype(jnp.bfloat16)
-    flipped = dot_nt(identity, received)
+    flipped = dot_nt(t_high[...], received)
     block_turned[...] = flipped.astype(jnp.bfloat16)
 
     def oriented(which):
@@ -427,8 +427,8 @@
 
 
 OLD_PIECES = ((0, 128, 384, 256, 128), (1, 384, 128, 256, 640), (0, 0, 128, 128, 0), (1, 256, 128, 128, 512))
-CROSSINGS = (0, 3, 6, -6, -3)
-CHUNKS = 2
+CROSSINGS = (0, 1, 4, -4, -1)
+CHUNKS = 4
 
 
 def place_kernel(dir_ref, stat_ref, moment_ref, dir_out, stat_out, moment_out, sem):
@@ -445,7 +445,7 @@
 
 
 def on_device(grad, statistics, moment, assignment, newton_steps):
-    order = make_plan(CROSSINGS, CHUNKS)[0]
+    order = make_plan(CROSSINGS, CHUNKS, tz=2.62, ty=6.2, lz=2.2, ly=4.0)[0]
     anywhere = pl.BlockSpec(memory_space=pl.ANY)
     wide_16 = pltpu.VMEM((512, 512), jnp.bfloat16)
     wide_32 = pltpu.VMEM((512, 512), jnp.float32)

time: 95.6 us -> 94.9 us (level)
  the two profiles are of different devices: /device:TPU:16 before, /device:TPU:2 now
where the time goes in v4:
time: 94.9 us; the launch traced here: 94.8 us
  Pallas kernels  94.1 us (99%)
    pallas_call x1, Pallas kernels, on_device(): pl.pallas_call(functools.partial(step_kernel, order, CHUNKS), out_shape=(...  91.8 us
    pallas_call x1, Pallas kernels, on_device(): pl.pallas_call(place_kernel, out_shape=tuple((jax.ShapeDtypeStruct(result...  2.3 us

profile of v4, /device:TPU:2, one launch (start us, length us, event | category | flops | bytes accessed | tf_op | source)
XLA Modules:
  0.0 94.8 jit_solution(17348898309839182987)
XLA Ops:
  0.6 91.8 %shampoo_step.1 = (bf16[32,1,256,256]{3,2,1,0:T(8,128)(2,1)S(1)}, f32[1,512,256]{2,1,0:T(8,128)S(1)}, f32[1,256,256]{2,1,0:T(8,128)S(1)}) custom-call(s32[8]{0:T(128)} %assign_hbm.1, s32[8]{0:T(128)} %newton_hbm.1, bf16[8,16,512]{2,1,0:T(8,128)(2,1)} %grad_hbm.1, f32[1,512,256]{2,1,0:T(8,128)} %stat_ref.1, f32[1,256,256]{2,1,0:T(8,128)} %moment_hbm.1), custom_call_target="tpu_custom_call" | custom-call | tf_op jit(solution)/shard_map/shampoo_step/pallas_call | solution.py:453
  92.5 2.3 %place_results.1 = (bf16[32,1,256,256]{3,2,1,0:T(8,128)(2,1)}, f32[1,512,256]{2,1,0:T(8,128)}, f32[1,256,256]{2,1,0:T(8,128)}) custom-call(bf16[32,1,256,256]{3,2,1,0:T(8,128)(2,1)S(1)} %get-tuple-element.6.dir_ref, f32[1,512,256]{2,1,0:T(8,128)S(1)} %get-tuple-element.7.stat_ref, f32[1,256,256]{2,1,0:T(8,128)S(1)} %get-tuple-element.8.moment_ref), custom_call_target="tpu_custom_call" | custom-call | tf_op jit(solution)/shard_map/place_results/pallas_call | solution.py:504
